TPU v7x, 32 devices: a whole 2x2x4 slice. The times are simulated.
32 devices in a mesh: fsdp: 8 (over z, core), grp: 2 (over y), tp: 2 (over x).
Axes of the slice: x: 2, y: 2, z: 4, core: 2. Of those that a mesh axis runs over, the one named last changes fastest.
Arguments:
- hidden_states: bfloat16 [4, 128, 8192], P(None, ('fsdp', 'grp'), 'tp'), may hold values from -6 to 6
- queries: bfloat16 [4, 128, 64, 128], P(None, ('fsdp', 'grp'), 'tp'), as said below
- cache_keys: bfloat16 [128, 768, 8, 128], P(('fsdp', 'grp'), None, 'tp'), as said below
- cache_values: bfloat16 [128, 768, 8, 128], P(('fsdp', 'grp'), None, 'tp'), may hold values from -6 to 6
- cache_lengths: int32 [128], P(('fsdp', 'grp')), may hold values from 2 to 768, as said below
- projection_weight_matrices: bfloat16 [2, 8192, 1024], P(None, None, 'tp'), may hold values from -0.0625 to 0.0625
- factor_down: bfloat16 [2, 8192, 64], P(None, ('fsdp', 'grp')), may hold values from -0.0625 to 0.0625
- factor_up: bfloat16 [2, 64, 1024], P(None, None, ('fsdp', 'grp')), may hold values from -0.375 to 0.375
Outputs:
- merged: bfloat16 [2, 8192, 1024], P(None, None, 'tp')
- attended: bfloat16 [4, 128, 64, 128], P(None, ('fsdp', 'grp'), 'tp')
Inputs may be any that keep to these rules, and one draw needn't show every extreme that they name: `cache_lengths`: at least 2; some row has exactly 768. `queries`: real-valued. `cache_keys`: real-valued.
All inputs are finite; a program needn't handle non-finite values.
Results may differ from a plain program's by a relative error of at most 0.0066.
Values may be sent and summed in bfloat16 or wider, within the bound.
No kernel may reach another device: no remote copies, remote signals or barrier semaphores. Data moves between devices by JAX's collectives and lax.ppermute only.
A program may use at most 192 MiB of HBM per device.

v0:
```python
import functools
import math

import jax
import jax.numpy as jnp
from jax import lax
from jax.experimental import pallas as pl
from jax.experimental.pallas import tpu as pltpu
from jax.sharding import PartitionSpec as P

AXES = ("fsdp", "grp", "tp")
ADAPTER_SCALING = 2.0
LOG2E = math.log2(math.e)
MIB = 1024 * 1024
ANY = pl.BlockSpec(memory_space=pl.ANY)
HBM = pl.BlockSpec(memory_space=pltpu.HBM)
VMEM = pl.BlockSpec(memory_space=pltpu.VMEM)
SMEM = pl.BlockSpec(memory_space=pltpu.SMEM)


class Layout:
    def __init__(self, mesh):
        self.fsdp, self.grp, self.tp = (mesh.shape[a] for a in AXES)
        self.depth = self.fsdp // 2
        self.ring = self.depth * self.grp
        self.block = self.depth // self.tp

    def flat(self, z, core, g, t):
        return ((z * 2 + core) * self.grp + g) * self.tp + t

    def devices(self):
        for z in range(self.depth):
            for core in range(2):
                for g in range(self.grp):
                    for t in range(self.tp):
                        yield z, core, g, t

    def place(self, z, g):
        return g * self.depth + (z if g % 2 == 0 else self.depth - 1 - z)

    def at(self, position):
        g, z = divmod(position, self.depth)
        return (z if g % 2 == 0 else self.depth - 1 - z), g

    def ring_step(self):
        pairs = []
        for z, core, g, t in self.devices():
            to_z, to_g = self.at((self.place(z, g) + (1 - 2 * core)) % self.ring)
            pairs.append((self.flat(z, core, g, t), self.flat(to_z, core, to_g, t)))
        return pairs

    def core_swap(self):
        return [
            (self.flat(z, c, g, t), self.flat(z, 1 - c, g, t)) for z, c, g, t in self.devices()
        ]

    def feature_step(self, step):
        return [
            (self.flat(z, c, g, (t + step) % self.tp), self.flat(z, c, g, t))
            for z, c, g, t in self.devices()
        ]

    def column_step(self, turn):
        pairs = []
        for z, c, g, t in self.devices():
            shift, turn_g = divmod(2 * turn + c, self.grp)
            source = t * self.block + (z % self.block + shift) % self.block
            pairs.append(
                (
                    self.flat(source, c, (g + turn_g) % self.grp, z // self.block),
                    self.flat(z, c, g, t),
                )
            )
        return pairs


def over(x, n):
    return x >> (n.bit_length() - 1) if n & (n - 1) == 0 else x // n


def within(x, n):
    return x & (n - 1) if n & (n - 1) == 0 else x % n


def after_all(arrays, token):
    return lax.optimization_barrier((arrays, token))


def pinned(x, space=pltpu.HBM):
    return pltpu.with_memory_space_constraint(x, space)


def sort_rows(lengths, order):
    rows = lengths.shape[0]
    held = [lengths[r] for r in range(rows)]
    for r in range(rows):
        rank = jnp.int32(0)
        for other in range(rows):
            if other != r:
                ahead = held[other] >= held[r] if other < r else held[other] > held[r]
                rank = rank + ahead.astype(jnp.int32)
        order[rank] = r


def by_length(length, sizes, act):
    below = 0
    for slots in sizes:

        @pl.when((length > below) & (length <= slots))
        def _():
            act(slots)

        below = slots


def cache_copies(first, spot, slots, kv, order, hbms, bufs, sems):
    span = pl.ds(0, slots * kv)
    return [
        [
            pltpu.make_async_copy(
                hbm.at[order[first + i], span], buf.at[spot + i, span], sems.at[i, which]
            )
            for which, (hbm, buf) in enumerate(zip(hbms, bufs))
        ]
        for i in range(2)
    ]


def begin_blocks(sizes, kv, len_hbm, q_hbm, k_hbm, v_hbm, *refs):
    len_ref, order, q_ref, k_ref, v_ref, sems, kv_sems = refs
    len_copy = pltpu.make_async_copy(len_hbm, len_ref, sems.at[0])
    q_copy = pltpu.make_async_copy(q_hbm, q_ref, sems.at[1])
    len_copy.start()
    q_copy.start()
    len_copy.wait()
    sort_rows(len_ref, order)

    def bring(slots):
        made = cache_copies(0, 0, slots, kv, order, (k_hbm, v_hbm), (k_ref, v_ref), kv_sems)
        for copies in made:
            for copy in copies:
                copy.start()
        for copies in made:
            for copy in copies:
                copy.wait()

    by_length(len_ref[order[0]], sizes, bring)
    q_copy.wait()


def begin(lengths, queries, keys, values, sizes, kv):
    rows = lengths.shape[0]
    buffer = pltpu.VMEM((rows // 2,) + keys.shape[1:], keys.dtype)
    return pl.pallas_call(
        functools.partial(begin_blocks, sizes, kv),
        out_shape=(
            pltpu.SMEM((rows,), jnp.int32),
            pltpu.SMEM((rows,), jnp.int32),
            pltpu.VMEM(queries.shape, queries.dtype),
            buffer,
            buffer,
        ),
        in_specs=[HBM] * 4,
        out_specs=(SMEM, SMEM, VMEM, VMEM, VMEM),
        scratch_shapes=[pltpu.SemaphoreType.DMA((2,)), pltpu.SemaphoreType.DMA((2, 2))],
        compiler_params=pltpu.CompilerParams(vmem_limit_bytes=8 * MIB),
        cost_estimate=pl.CostEstimate(
            flops=0, bytes_accessed=8 * keys[0].size, transcendentals=0
        ),
        name="begin",
    )(pinned(lengths), pinned(queries), pinned(keys), pinned(values))


def pack_pair(own_hbm, other, own_up, other_up, *refs):
    pair, up_pair, sems = refs[-3:]
    core = lax.rem(lax.axis_index("fsdp"), 2)
    copies = [
        pltpu.make_async_copy(own_hbm, pair.at[core], sems.at[0]),
        pltpu.make_async_copy(other, pair.at[1 - core], sems.at[1]),
    ]
    for copy in copies:
        copy.start()
    for ref, place in ((own_up, core), (other_up, 1 - core)):
        up_pair[place] = jnp.concatenate([ref[k] for k in range(ref.shape[0])], axis=1)
    for copy in copies:
        copy.wait()


def pack(own, other, own_up, other_up, after):
    count, rank, columns = own_up.shape
    return pl.pallas_call(
        pack_pair,
        out_shape=(
            pltpu.VMEM((2,) + own.shape, own.dtype),
            pltpu.VMEM((2, rank, count * columns), own.dtype),
        ),
        in_specs=[HBM, ANY, VMEM, VMEM] + [ANY] * len(after),
        out_specs=(VMEM, VMEM),
        scratch_shapes=[pltpu.SemaphoreType.DMA((2,))],
        compiler_params=pltpu.CompilerParams(vmem_limit_bytes=4 * MIB),
        name="pack_pair",
    )(pinned(own), other, own_up, other_up, *after)


def attend_cache(part, pairs, sizes, scale, n_kept, *refs):
    lengths, order, q_ref, k_hbm, v_hbm, w_hbm = refs[:6]
    sems, w_sem = refs[-2:]
    k_buf, v_buf, w_ref, o_ref, lse_ref = refs[-7 - n_kept : -2 - n_kept]
    steps, _, heads, size = q_ref.shape
    kv = k_hbm.shape[1] // sizes[-1]
    lanes = steps * heads
    brought = 1 if part == 0 else 0

    def copies(pair, slots):
        first = 2 * (part * pairs + pair)
        return cache_copies(
            first, 2 * pair, slots, kv, order, (k_hbm, v_hbm), (k_buf, v_buf), sems.at[pair]
        )

    def start(pair, slots):
        for made in copies(pair, slots):
            for copy in made:
                copy.start()

    for pair in range(brought, pairs):
        length = lengths[order[2 * (part * pairs + pair)]]
        by_length(length, sizes, functools.partial(start, pair))
    w_copy = pltpu.make_async_copy(w_hbm.at[part], w_ref, w_sem)
    w_copy.start()

    row_head = over(within(lax.broadcasted_iota(jnp.int32, (lanes, size), 0), heads), heads // kv)
    slot_head = within(lax.broadcasted_iota(jnp.int32, (lanes, size), 1), kv)
    head_bias = jnp.where(row_head == slot_head, 0.0, -jnp.inf)

    @pl.loop(0, pairs)
    def _(pair):
        first = 2 * (part * pairs + pair)

        def compute(slots):
            waits = copies(pair, slots)

            def wait(which):
                @pl.when(pair >= brought)
                def _():
                    for made in waits:
                        made[which].wait()

            n = slots * kv
            bias = jnp.concatenate([head_bias[:, : min(n, size)]] * max(n // size, 1), axis=1)
            column = lax.broadcasted_iota(jnp.int32, (1, n), 1)
            wait(0)
            wait(1)
            scores = []
            for i in range(2):
                row = order[first + i]
                q = q_ref[:, row].reshape(lanes, size)
                s = lax.dot_general(
                    q,
                    k_buf[2 * pair + i, :n],
                    (((1,), (1,)), ((), ())),
                    preferred_element_type=jnp.float32,
                )
                closed = jnp.where(column < lengths[row] * kv, 0.0, -jnp.inf)
                scores.append(s + (bias + closed))
            highest = [jnp.max(s, axis=1, keepdims=True) * scale for s in scores]
            weights = [jnp.exp2(s * scale - h) for s, h in zip(scores, highest)]
            totals = [jnp.sum(p, axis=1, keepdims=True) for p in weights]
            for i in range(2):
                spot = 2 * pair + i
                o = jnp.dot(
                    weights[i].astype(jnp.bfloat16),
                    v_buf[spot, :n],
                    preferred_element_type=jnp.float32,
                )
                o_ref[spot] = o / totals[i]
                lse = highest[i] + jnp.log(totals[i]) * LOG2E
                lse_ref[spot] = jnp.broadcast_to(lse, (lanes, size))

        by_length(lengths[order[first]], sizes, compute)

    w_copy.wait()


def cache_attention(part, lengths, order, queries, keys, values, weights, buffers, kept, sizes, after):
    steps, rows, heads, size = queries.shape
    pairs = rows // 4
    slots = sizes[-1]
    kv = keys.shape[1] // slots
    scale = LOG2E / math.sqrt(size)
    piece = pltpu.VMEM((2 * pairs, steps * heads, size), jnp.float32)
    operands = [pinned(lengths, pltpu.SMEM), pinned(order, pltpu.SMEM), pinned(queries, pltpu.VMEM)]
    operands += [pinned(keys), pinned(values), pinned(weights)]
    specs = [SMEM, SMEM, VMEM, HBM, HBM, HBM]
    at = len(operands)
    aliases = {at: 0, at + 1: 1} | {at + 2 + i: 5 + i for i in range(len(kept))}
    operands += [pinned(b, pltpu.VMEM) for b in buffers + kept] + after
    specs += [VMEM] * (len(buffers) + len(kept)) + [ANY] * len(after)

    def like(x):
        return pltpu.VMEM(x.shape, x.dtype)

    return pl.pallas_call(
        functools.partial(attend_cache, part, pairs, sizes, scale, len(kept)),
        out_shape=(
            *(like(b) for b in buffers),
            pltpu.VMEM(weights.shape[1:], weights.dtype),
            piece,
            piece,
            *(like(x) for x in kept),
        ),
        in_specs=specs,
        out_specs=(VMEM,) * (5 + len(kept)),
        input_output_aliases=aliases,
        scratch_shapes=[
            pltpu.SemaphoreType.DMA((pairs, 2, 2)),
            pltpu.SemaphoreType.DMA,
        ],
        compiler_params=pltpu.CompilerParams(vmem_limit_bytes=16 * MIB),
        cost_estimate=pl.CostEstimate(
            flops=8 * steps * heads * pairs * slots * kv * size,
            bytes_accessed=8 * pairs * slots * kv * size + 2 * weights[0].size,
            transcendentals=2 * steps * heads * pairs * slots * kv,
        ),
        name="cache_attention",
    )(*operands)


def merge_blocks(lay, plan, counts, first, last, scale, *refs):
    refs = list(refs)

    def take(n):
        out = refs[:n]
        del refs[:n]
        return out

    take(2)
    downs = take(len(plan))
    if first:
        hidden, ups = take(counts[0]), take(counts[1])
    else:
        u_in, h_in, _, fresh_in, low_in = take(5)
    if last:
        order, q_ref = take(2)
        caches = [take(2) for _ in range(2)]
    take(len(refs) - (4 if last else 5) - (3 if first else 0) - 2 - (2 if last else 0))
    m_hbm, *weights = take(3)
    (out_ref,) = take(1) if last else (None,)
    if first:
        u_buf, h_buf = take(2)
    else:
        u_buf, h_buf = u_in, h_in
    if last:
        fresh, low = refs[-2:]
        del refs[-2:]
    else:
        fresh, low = take(2)
    if first:
        u_parts = refs.pop()
    m_buf, sems = refs

    pairs, depth, width = m_buf.shape[1:]
    cut = min(width, 256)
    fsdp, grp, tp = (lax.axis_index(a) for a in AXES)
    z, core = fsdp // 2, lax.rem(fsdp, 2)
    place = grp * lay.depth + jnp.where(lax.rem(grp, 2) == 0, z, lay.depth - 1 - z)
    per_lane = lay.fsdp * lay.grp // lay.tp

    if first:
        for i, h in enumerate(hidden):
            h_buf[lax.rem(tp + i, lay.tp)] = h[...]
        for i, up in enumerate(ups):
            flip, turn = divmod(i, len(ups) // 2)
            spot = 2 * turn + (1 - core if flip else core)
            shift, turn = spot // lay.grp, lax.rem(spot, lay.grp)
            zz = lax.rem(lax.rem(z, lay.block) + shift, lay.block)
            for c in range(2):
                u_parts[(zz * 2 + c) * lay.grp + lax.rem(grp + turn, lay.grp)] = up[c]
        columns = u_parts.shape[2] // pairs
        for k in range(pairs):
            u_buf[k] = ADAPTER_SCALING * jnp.concatenate(
                [u_parts[i, :, k * columns : (k + 1) * columns] for i in range(u_parts.shape[0])],
                axis=1,
            )
        fresh[...] = jnp.zeros_like(fresh)
        low[...] = jnp.zeros_like(low)
    else:
        fresh[...] = fresh_in[...]
        low[...] = low_in[...]

    chunk = min(depth, 256)
    j = 0
    for (step, flip, whole), down in zip(plan, downs):
        towards = 2 * core - 1
        spot = lax.rem(place + lay.ring + step * (-towards if flip else towards), lay.ring)
        g = spot // lay.depth
        along = lax.rem(spot, lay.depth)
        zz = jnp.where(lax.rem(g, 2) == 0, along, lay.depth - 1 - along)
        def block(c, j=j, down=down, flip=flip, whole=whole, zz=zz):
            cc = c if whole else (1 - core if flip else core)
            index = (zz * 2 + cc) * lay.grp + g
            start = pl.multiple_of(index * depth, depth)
            column = pl.multiple_of(lax.rem(index, per_lane) * depth, depth)
            source = index // per_lane
            for k in range(pairs):
                for begin in range(0, depth, chunk):
                    rows = slice(begin, begin + chunk)
                    d = down[c, k, :, rows]
                    h = h_buf[source, :, pl.ds(column + begin, chunk)]
                    for side in range(width // cut):
                        cols = slice(side * cut, (side + 1) * cut)
                        w = weights[k][pl.ds(start + begin, chunk), cols]
                        added = lax.dot_general(
                            d,
                            u_buf[k, :, cols],
                            (((0,), (0,)), ((), ())),
                            preferred_element_type=jnp.float32,
                        )
                        m_buf[j + c, k, rows, cols] = (w.astype(jnp.float32) + added).astype(
                            jnp.bfloat16
                        )
                        fresh[k, :, cols] += jnp.dot(h, w, preferred_element_type=jnp.float32)
                    low[k] += lax.dot_general(
                        h, d, (((1,), (1,)), ((), ())), preferred_element_type=jnp.float32
                    )
                pltpu.make_async_copy(
                    m_buf.at[j + c, k], m_hbm.at[k, pl.ds(start, depth), :], sems.at[j + c, k]
                ).start()

        if down.shape[0] == 1:
            block(0)
        else:
            pl.loop(0, down.shape[0])(block)
        j += down.shape[0]

    if last:
        new = []
        for k in range(pairs):
            high = low[k].astype(jnp.bfloat16)
            rest = (low[k] - high.astype(jnp.float32)).astype(jnp.bfloat16)
            new.append(
                (
                    fresh[k]
                    + jnp.dot(high, u_buf[k], preferred_element_type=jnp.float32)
                    + jnp.dot(rest, u_buf[k], preferred_element_type=jnp.float32)
                ).astype(jnp.bfloat16)
            )
        add_new_tokens(q_ref, order, caches, new, out_ref, scale)
    for i in range(j):
        for k in range(pairs):
            pltpu.make_async_copy(
                m_buf.at[i, k], m_hbm.at[k, pl.ds(0, depth), :], sems.at[i, k]
            ).wait()


def add_new_tokens(q_ref, order, caches, new, out_ref, scale):
    steps, rows, heads, size = q_ref.shape
    kv = new[0].shape[1] // size
    new = [
        jnp.concatenate([x[:, g * size : (g + 1) * size] for g in range(kv)], axis=0) for x in new
    ]
    n = kv * steps * rows
    lanes = steps * heads
    left = lax.broadcasted_iota(jnp.int32, (lanes, n), 0)
    right = lax.broadcasted_iota(jnp.int32, (lanes, n), 1)
    same_head = over(within(left, heads), heads // kv) == over(right, steps * rows)
    earlier = within(over(right, rows), steps) <= over(left, heads)
    right_row = jnp.where(same_head & earlier, within(right, rows), -1)
    spots = [(o, lse, i) for o, lse in caches for i in range(o.shape[0])]
    for spot, (o_ref, lse_ref, i) in enumerate(spots):
        row = order[spot]
        q = q_ref[:, row].reshape(lanes, size)
        s = lax.dot_general(
            q, new[0], (((1,), (1,)), ((), ())), preferred_element_type=jnp.float32
        )
        s = jnp.where(right_row == row, s * scale, -jnp.inf)
        lse = lse_ref[i]
        highest = jnp.maximum(jnp.max(s, axis=1, keepdims=True), lse)
        p = jnp.exp2(s - highest[:, :n])
        old = jnp.exp2(lse - highest)
        divisor = jnp.sum(p, axis=1, keepdims=True) + old
        o = old * o_ref[i] + jnp.dot(
            p.astype(jnp.bfloat16), new[1], preferred_element_type=jnp.float32
        )
        out_ref[:, row] = (o / divisor).reshape(steps, heads, size).astype(out_ref.dtype)


def merge(lay, shape, entries, weights, inputs, state, final, after):
    pairs, total, width = shape
    rank, depth = entries[0][3].shape[2:]
    first, last = state is None, final is not None
    n = sum(e[3].shape[0] for e in entries)
    operands = [pinned(w, pltpu.VMEM) for w in weights] + [e[3] for e in entries]
    specs = [VMEM] * len(operands)
    counts = (0, 0)
    aliases = {0: 1, 1: 2}
    if first:
        hidden, ups = inputs
        counts = (len(hidden), len(ups))
        operands += hidden + ups
        specs += [VMEM] * (len(hidden) + len(ups))
        tokens, features = hidden[0].shape
    else:
        m_prev, u, h, fresh, low = state
        aliases[len(operands) + 2] = 0
        operands += [u, h, pinned(m_prev), fresh, low]
        specs += [VMEM, VMEM, HBM, VMEM, VMEM]
        tokens = h.shape[1]
    out_shape = [pltpu.HBM(shape, jnp.bfloat16)]
    out_shape += [pltpu.VMEM(w.shape, w.dtype) for w in weights]
    sums = [(pairs, tokens, width), (pairs, tokens, rank)]
    scratch = [
        pltpu.VMEM((n, pairs, depth, width), jnp.bfloat16),
        pltpu.SemaphoreType.DMA((n, 2)),
    ]
    scale = 0.0
    if first:
        out_shape += [
            pltpu.VMEM(s, jnp.bfloat16)
            for s in ((pairs, rank, width), (lay.tp, tokens, features))
        ]
        parts = len(ups) * 2
        scratch.append(pltpu.VMEM((parts,) + ups[0].shape[1:], jnp.bfloat16))
    if last:
        order, queries, caches = final
        operands += [pinned(order, pltpu.SMEM), pinned(queries, pltpu.VMEM)] + caches
        specs += [SMEM] + [VMEM] * (1 + len(caches))
        out_shape.append(jax.ShapeDtypeStruct(queries.shape, jnp.bfloat16))
        scale = LOG2E / math.sqrt(queries.shape[3])
        scratch += [pltpu.VMEM(s, jnp.float32) for s in sums]
    else:
        out_shape += [pltpu.VMEM(s, jnp.float32) for s in sums]
    operands += after
    specs += [ANY] * len(after)
    out = pl.pallas_call(
        functools.partial(
            merge_blocks, lay, [e[:3] for e in entries], counts, first, last, scale
        ),
        out_shape=out_shape,
        in_specs=specs,
        out_specs=[HBM] + [VMEM] * (len(out_shape) - 1),
        input_output_aliases=aliases,
        scratch_shapes=scratch,
        compiler_params=pltpu.CompilerParams(vmem_limit_bytes=14 * MIB),
        cost_estimate=pl.CostEstimate(
            flops=2 * n * pairs * depth * width * (rank + tokens),
            bytes_accessed=2 * n * pairs * depth * width,
            transcendentals=0,
        ),
        name="merge_blocks",
    )(*operands)
    out, weights = [out[0], *out[3:]], out[1:3]
    if not last and not first:
        out = [out[0], u, h, *out[1:]]
    return out, weights


def shards(
    lay,
    hidden_states,
    queries,
    cache_keys,
    cache_values,
    cache_lengths,
    projection_weight_matrices,
    factor_down,
    factor_up,
):
    send = functools.partial(lax.ppermute, axis_name=AXES)
    steps, rows, features = hidden_states.shape
    slots, kv, size = cache_keys.shape[1:]
    shape = projection_weight_matrices.shape
    sizes = tuple(slots * i // 24 for i in (1, 4, 8, 16, 24))
    own = jnp.swapaxes(factor_down, 1, 2)
    tokens = hidden_states.reshape(steps * rows, features)
    keys = cache_keys.reshape(rows, slots * kv, size)
    values = cache_values.reshape(rows, slots * kv, size)
    swap, ring = lay.core_swap(), lay.ring_step()
    caches = []

    other, other_up = send(own, perm=swap), send(factor_up, perm=swap)
    lengths, order, q, *buffers = begin(cache_lengths, queries, keys, values, sizes, kv)
    pair, up_pair = pack(own, other, factor_up, other_up, [q])

    def attention(part, buffers, kept, after):
        out = cache_attention(
            part,
            lengths,
            order,
            q,
            keys,
            values,
            projection_weight_matrices,
            list(buffers),
            list(kept),
            sizes,
            after,
        )
        caches.extend(out[3:5])
        return out[:2], [*out[5:], out[2]]

    ups = [
        send(up_pair, perm=lay.column_step(turn)) for turn in range(lay.block * lay.grp // 2)
    ]
    came = send(pair, perm=ring)
    buffers, weights = attention(0, buffers, [], [pair])
    (came, ups, tokens), token = after_all((came, ups, tokens), caches[0])

    sent = send(came, perm=ring)
    swapped = send(came, perm=swap)
    other_ups = [send(u, perm=swap) for u in ups]
    hidden = [send(tokens, perm=lay.feature_step(i)) for i in range(1, lay.tp)]
    buffers, weights = attention(1, buffers, weights, [token])
    (sent, swapped, other_ups, hidden), token = after_all(
        (sent, swapped, other_ups, hidden), caches[2]
    )
    entries = [(0, False, True, pair), (1, False, True, came), (1, True, True, swapped)]
    came = sent

    inputs = ([tokens] + hidden, ups + other_ups)
    state = None
    last_step = lay.ring // 2
    for step in range(2, last_step):
        if step + 1 < last_step:
            sent = send(came, perm=ring)
        else:
            core = lax.rem(lax.axis_index("fsdp"), 2)
            sent = send(lax.dynamic_slice_in_dim(came, core, 1, 0), perm=ring)
        swapped = send(came, perm=swap)
        state, weights = merge(lay, shape, entries, weights, inputs, state, None, [token])
        (sent, swapped), token = after_all((sent, swapped), state[3])
        entries = [(step, False, True, came), (step, True, True, swapped)]
        came = sent
    swapped = send(came, perm=swap)
    entries.append((last_step, False, False, came))
    state, weights = merge(lay, shape, entries, weights, inputs, state, None, [token])
    entries = [(last_step, True, False, swapped)]
    out, _ = merge(lay, shape, entries, weights, inputs, state, (order, q, caches), [])
    return tuple(out)


def solution(mesh):
    return jax.shard_map(
        functools.partial(shards, Layout(mesh)),
        mesh=mesh,
        in_specs=(
            P(None, ("fsdp", "grp"), "tp"),
            P(None, ("fsdp", "grp"), "tp", None),
            P(("fsdp", "grp"), None, "tp", None),
            P(("fsdp", "grp"), None, "tp", None),
            P(("fsdp", "grp")),
            P(None, None, "tp"),
            P(None, ("fsdp", "grp"), None),
            P(None, None, ("fsdp", "grp")),
        ),
        out_specs=(P(None, None, "tp"), P(None, ("fsdp", "grp"), "tp", None)),
        check_vma=False,
    )
```

profile of v0, /device:TPU:0, one launch (start us, length us, event | category | flops | bytes accessed | tf_op | source)
XLA Modules:
  0.0 74.4 jit_solution(9968007910314372098)
XLA Ops:
  0.6 0.0 copy-start.9
  0.6 0.5 collective-permute-start
  1.2 0.1 collective-permute-start.1
  1.2 2.7 %begin.1 = (s32[8]{0:T(128)S(4)}, s32[8]{0:T(128)S(4)}, bf16[4,8,32,128]{3,2,1,0:T(8,128)(2,1)S(1)}, bf16[4,3072,128]{2,1,0:T(8,128)(2,1)S(1)}, bf16[4,3072,128]{2,1,0:T(8,128)(2,1)S(1)}) custom-call(s32[8]{0:T(128)} %len_hbm.1, bf16[4,8,32,128]{3,2,1,0:T(8,128)(2,1)} %q_hbm.1, bf16[8,3072,128]{2,1,0:T(8,128)(2,1)} %bitcast.6, bf16[8,3072,128]{2,1,0:T(8,128)(2,1)} %bitcast.9), custom_call_target="tpu_custom_call" | custom-call | bytes 3145728 | tf_op jit(solution)/shard_map/begin/pallas_call | solution.py:154
  4.0 0.0 collective-permute-done.1.other_up
  4.0 0.0 collective-permute-done.other
  4.0 0.0 copy-done.9
  4.0 0.9 %pack_pair.1 = (bf16[2,2,64,512]{3,2,1,0:T(8,128)(2,1)S(1)}, bf16[2,64,128]{2,1,0:T(8,128)(2,1)S(1)}) custom-call(bf16[2,64,512]{2,1,0:T(8,128)(2,1)} %bitcast.13, bf16[2,64,512]{2,1,0:T(8,128)(2,1)S(1)} %collective-permute-done.other, bf16[2,64,64]{2,1,0:T(8,128)(2,1)S(1)} %copy-done.9, bf16[2,64,64]{2,1,0:T(8,128)(2,1)S(1)} %collective-permute-done.1.other_up, ...), custom_call_target="tpu_custom_call" | custom-call | tf_op jit(solution)/shard_map/pack_pair/pallas_call | solution.py:191
  4.9 3.1 %collective-permute-start.2 = (bf16[2,2,64,512]{3,2,1,0:T(8,128)(2,1)S(1)}, bf16[2,2,64,512]{3,2,1,0:T(8,128)(2,1)S(1)}, u32[]{:S(2)}, u32[]{:S(2)}) collective-permute-start(bf16[2,2,64,512]{3,2,1,0:T(8,128)(2,1)S(1)} %get-tuple-element.59.refs_8_.refs_2_), channel_id=1, source_target_pairs={{0,8},{1,9},{2,0},{3,1},{4,6},{5,7},{6,14},{7,15},{8,16},{9,17},{1... | collective-permute-start | bytes 786440 | tf_op jit(solution)/shard_map/ppermute | solution.py:604
  8.0 0.7 collective-permute-start.3
  8.7 1.2 %collective-permute-start.4 = (bf16[2,64,128]{2,1,0:T(8,128)(2,1)S(1)}, bf16[2,64,128]{2,1,0:T(8,128)(2,1)S(1)}, u32[]{:S(2)}, u32[]{:S(2)}) collective-permute-start(bf16[2,64,128]{2,1,0:T(8,128)(2,1)S(1)} %get-tuple-element.63), channel_id=1, source_target_pairs={{8,0},{24,1},{10,2},{26,3},{14,4},{30,5},{12,6},{28,7},{0,8},{16,9... | collective-permute-start | bytes 98312 | tf_op jit(solution)/shard_map/ppermute | solution.py:602
  10.0 5.1 %cache_attention.2 = (bf16[4,3072,128]{2,1,0:T(8,128)(2,1)S(1)}, bf16[4,3072,128]{2,1,0:T(8,128)(2,1)S(1)}, bf16[8192,512]{1,0:T(8,128)(2,1)S(1)}, f32[4,128,128]{2,1,0:T(8,128)S(1)}, f32[4,128,128]{2,1,0:T(8,128)S(1)}) custom-call(s32[8]{0:T(128)S(4)} %get-tuple-element.54.refs_0_, ...), custom_call_target="tpu_custom_call", output_to_operand_aliasing={{0}: (6, {}), {1}: (7, {})} | custom-call | flops 805306368 | bytes 14680064 | tf_op jit(solution)/shard_map/cache_attention/pallas_call | solution.py:302
  15.1 0.0 collective-permute-done.3.refs_7_
  15.1 0.0 collective-permute-done.4.refs_8_
  15.1 0.0 collective-permute-done.2.refs_3_
  15.1 0.1 collective-permute-start.5
  15.2 3.5 %collective-permute-start.6 = (bf16[2,2,64,512]{3,2,1,0:T(8,128)(2,1)S(1)}, bf16[2,2,64,512]{3,2,1,0:T(8,128)(2,1)S(1)}, u32[]{:S(2)}, u32[]{:S(2)}) collective-permute-start(bf16[2,2,64,512]{3,2,1,0:T(8,128)(2,1)S(1)} %collective-permute-done.2.refs_3_), channel_id=1, source_target_pairs={{0,4},{1,5},{2,6},{3,7},{4,0},{5,1},{6,2},{7,3},{8,12},{9,13},{10,... | collective-permute-start | bytes 786440 | tf_op jit(solution)/shard_map/ppermute | solution.py:609
  18.7 4.2 %collective-permute-start.9 = (bf16[32,4096]{1,0:T(8,128)(2,1)S(1)}, bf16[32,4096]{1,0:T(8,128)(2,1)S(1)}, u32[]{:S(2)}, u32[]{:S(2)}) collective-permute-start(bf16[32,4096]{1,0:T(8,128)(2,1)S(1)} %bitcast.4), channel_id=1, source_target_pairs={{1,0},{0,1},{3,2},{2,3},{5,4},{4,5},{7,6},{6,7},{9,8},{8,9},{11,10... | collective-permute-start | bytes 786440 | tf_op jit(solution)/shard_map/ppermute | solution.py:611
  22.9 0.0 collective-permute-start.7
  22.9 0.5 collective-permute-start.8
  23.4 3.6 %cache_attention.3 = (bf16[4,3072,128]{2,1,0:T(8,128)(2,1)S(1)}, bf16[4,3072,128]{2,1,0:T(8,128)(2,1)S(1)}, bf16[8192,512]{1,0:T(8,128)(2,1)S(1)}, f32[4,128,128...) custom-call(s32[8]{0:T(128)S(4)} %get-tuple-element.54.refs_0_, ...), custom_call_target="tpu_custom_call", output_to_operand_aliasing={{0}: (6, {}), {1}: (7, {}), {5}: (8, {})} | custom-call | flops 805306368 | bytes 14680064 | tf_op jit(solution)/shard_map/cache_attention/pallas_call | solution.py:302
  27.0 0.0 collective-permute-done.7.refs_9_
  27.0 0.0 collective-permute-done.8.refs_10_
  27.0 0.0 collective-permute-done.5.refs_2_
  27.0 0.0 collective-permute-done.6.refs_4_
  27.1 2.3 %collective-permute-done.9.refs_6_ = bf16[32,4096]{1,0:T(8,128)(2,1)S(1)} collective-permute-done((bf16[32,4096]{1,0:T(8,128)(2,1)S(1)}, bf16[32,4096]{1,0:T(8,128)(2,1)S(1)}, u32[]{:S(2)}, u32[]{:S(2)}) %collective-permute-start.9) | collective-permute-done | bytes 262176 | tf_op jit(solution)/shard_map/ppermute | solution.py:611
  29.3 0.9 %collective-permute-start.10 = (bf16[2,2,64,512]{3,2,1,0:T(8,128)(2,1)S(1)}, bf16[2,2,64,512]{3,2,1,0:T(8,128)(2,1)S(1)}, u32[]{:S(2)}, u32[]{:S(2)}) collective-permute-start(bf16[2,2,64,512]{3,2,1,0:T(8,128)(2,1)S(1)} %collective-permute-done.5.refs_2_), channel_id=1, source_target_pairs={{0,8},{1,9},{2,0},{3,1},{4,6},{5,7},{6,14},{7,15},{8,16},{9,17},{1... | collective-permute-start | bytes 786440 | tf_op jit(solution)/shard_map/ppermute | solution.py:624
  30.2 0.0 collective-permute-start.11
  30.2 4.4 %merge_blocks.4 = (bf16[2,8192,512]{2,1,0:T(8,128)(2,1)}, bf16[8192,512]{1,0:T(8,128)(2,1)S(1)}, bf16[8192,512]{1,0:T(8,128)(2,1)S(1)}, bf16[2,64,512]{2,1,0:T(8...) custom-call(bf16[8192,512]{1,0:T(8,128)(2,1)S(1)} %get-tuple-element, ...), custom_call_target="tpu_custom_call", output_to_operand_aliasing={{1}: (0, {}), {2}: (1, {})} | custom-call | flops 603979776 | bytes 6291456 | tf_op jit(solution)/shard_map/merge_blocks/pallas_call | solution.py:534
  34.6 3.3 %copy-done = bf16[8192,512]{1,0:T(8,128)(2,1)} copy-done((bf16[8192,512]{1,0:T(8,128)(2,1)}, bf16[8192,512]{1,0:T(8,128)(2,1)S(1)}, u32[]{:S(2)}) %copy-start) | copy-done | bytes 8388632
  37.9 3.2 %copy-done.4 = bf16[8192,512]{1,0:T(8,128)(2,1)} copy-done((bf16[8192,512]{1,0:T(8,128)(2,1)}, bf16[8192,512]{1,0:T(8,128)(2,1)S(1)}, u32[]{:S(2)}) %copy-start.4) | copy-done | bytes 8388632
  41.1 0.0 collective-permute-done.10.refs_2_
  41.1 0.0 collective-permute-done.11.refs_3_
  41.1 0.5 collective-permute-start.13
  41.6 2.4 %collective-permute-start.12 = (bf16[1,2,64,512]{3,2,1,0:T(8,128)(2,1)S(1)}, bf16[1,2,64,512]{3,2,1,0:T(8,128)(2,1)S(1)}, u32[]{:S(2)}, u32[]{:S(2)}) collective-permute-start(bf16[1,2,64,512]{3,2,1,0:T(8,128)(2,1)S(1)} %constant_dynamic-slice_fusion), channel_id=1, source_target_pairs={{0,8},{1,9},{2,0},{3,1},{4,6},{5,7},{6,14},{7,15},{8,16},{9,17},{1... | collective-permute-start | bytes 393224 | tf_op jit(solution)/shard_map/ppermute | solution.py:627
  44.0 3.4 %copy-done.1 = bf16[8192,512]{1,0:T(8,128)(2,1)S(1)} copy-done((bf16[8192,512]{1,0:T(8,128)(2,1)S(1)}, bf16[8192,512]{1,0:T(8,128)(2,1)}, u32[]{:S(2)}) %copy-start.1) | copy-done | bytes 8388632
  47.4 3.4 %copy-done.5 = bf16[8192,512]{1,0:T(8,128)(2,1)S(1)} copy-done((bf16[8192,512]{1,0:T(8,128)(2,1)S(1)}, bf16[8192,512]{1,0:T(8,128)(2,1)}, u32[]{:S(2)}) %copy-start.5) | copy-done | bytes 8388632
  50.8 3.1 %merge_blocks.5 = (bf16[2,8192,512]{2,1,0:T(8,128)(2,1)}, bf16[8192,512]{1,0:T(8,128)(2,1)S(1)}, bf16[8192,512]{1,0:T(8,128)(2,1)S(1)}, f32[2,32,512]{2,1,0:T(8,128)S(1)}, f32[2,32,64]{2,1,0:T(8,128)S(1)}) custom-call(bf16[8192,512]{1,0:T(8,128)(2,1)S(1)} %copy-done.1, ...), custom_call_target="tpu_custom_call", output_to_operand_aliasing={{1}: (0, {}), {2}: (1, {}), {0}: (6, {})} | custom-call | flops 402653184 | bytes 4194304 | tf_op jit(solution)/shard_map/merge_blocks/pallas_call | solution.py:534
  53.9 0.0 collective-permute-done.12.refs_4_
  53.9 0.0 collective-permute-done.13.refs_3_
  53.9 0.1 collective-permute-start.14
  54.0 3.7 %merge_blocks.6 = (bf16[2,8192,512]{2,1,0:T(8,128)(2,1)}, bf16[8192,512]{1,0:T(8,128)(2,1)S(1)}, bf16[8192,512]{1,0:T(8,128)(2,1)S(1)}, f32[2,32,512]{2,1,0:T(8,128)S(1)}, f32[2,32,64]{2,1,0:T(8,128)S(1)}) custom-call(bf16[8192,512]{1,0:T(8,128)(2,1)S(1)} %get-tuple-element.88.refs_0_, ...), custom_call_target="tpu_custom_call", output_to_operand_aliasing={{1}: (0, {}), {2}: (1, {}), {0}: (7, {})} | custom-call | flops 503316480 | bytes 5242880 | tf_op jit(solution)/shard_map/merge_blocks/pallas_call | solution.py:534
  57.7 3.3 %copy-done.2 = bf16[8192,512]{1,0:T(8,128)(2,1)} copy-done((bf16[8192,512]{1,0:T(8,128)(2,1)}, bf16[8192,512]{1,0:T(8,128)(2,1)S(1)}, u32[]{:S(2)}) %copy-start.2) | copy-done | bytes 8388632
  60.9 3.2 %copy-done.6 = bf16[8192,512]{1,0:T(8,128)(2,1)} copy-done((bf16[8192,512]{1,0:T(8,128)(2,1)}, bf16[8192,512]{1,0:T(8,128)(2,1)S(1)}, u32[]{:S(2)}) %copy-start.6) | copy-done | bytes 8388632
  64.2 0.0 collective-permute-done.14.refs_2_
  64.2 3.4 %copy-done.3 = bf16[8192,512]{1,0:T(8,128)(2,1)S(1)} copy-done((bf16[8192,512]{1,0:T(8,128)(2,1)S(1)}, bf16[8192,512]{1,0:T(8,128)(2,1)}, u32[]{:S(2)}) %copy-start.3) | copy-done | bytes 8388632
  67.5 3.4 %copy-done.7 = bf16[8192,512]{1,0:T(8,128)(2,1)S(1)} copy-done((bf16[8192,512]{1,0:T(8,128)(2,1)S(1)}, bf16[8192,512]{1,0:T(8,128)(2,1)}, u32[]{:S(2)}) %copy-start.7) | copy-done | bytes 8388632
  70.9 3.3 %merge_blocks.7 = (bf16[2,8192,512]{2,1,0:T(8,128)(2,1)}, bf16[8192,512]{1,0:T(8,128)(2,1)S(1)}, bf16[8192,512]{1,0:T(8,128)(2,1)S(1)}, bf16[4,8,32,128]{3,2,1,0:T(8,128)(2,1)}) custom-call(bf16[8192,512]{1,0:T(8,128)(2,1)S(1)} %copy-done.3, bf16[8192,512]{1,0:T(8,128)(2,1)S(1)} %copy-done.7, ...), custom_call_target="tpu_custom_call", output_to_operand_aliasing={{1}: (0, {}), {2}: (1, {}), {0}: (5, {})} | custom-call | flops 100663296 | bytes 1048576 | tf_op jit(solution)/shard_map/merge_blocks/pallas_call | solution.py:534
  (11 shorter events, 0.0 us)
Async XLA Ops:
  0.6 3.4 %copy-start.9 = (bf16[2,64,64]{2,1,0:T(8,128)(2,1)S(1)}, bf16[2,64,64]{2,1,0:T(8,128)(2,1)}, u32[]{:S(2)}) copy-start(bf16[2,64,64]{2,1,0:T(8,128)(2,1)} %own_up.1) | copy-start | bytes 49156
  0.6 3.3 %collective-permute-start = (bf16[2,64,512]{2,1,0:T(8,128)(2,1)}, bf16[2,64,512]{2,1,0:T(8,128)(2,1)S(1)}, u32[]{:S(2)}, u32[]{:S(2)}) collective-permute-start(bf16[2,64,512]{2,1,0:T(8,128)(2,1)} %bitcast.12), channel_id=1, source_target_pairs={{0,4},{1,5},{2,6},{3,7},{4,0},{5,1},{6,2},{7,3},{8,12},{9,13},{10,... | collective-permute-start | bytes 393224 | tf_op jit(solution)/shard_map/ppermute | solution.py:580
  1.2 2.8 %collective-permute-start.1 = (bf16[2,64,64]{2,1,0:T(8,128)(2,1)}, bf16[2,64,64]{2,1,0:T(8,128)(2,1)S(1)}, u32[]{:S(2)}, u32[]{:S(2)}) collective-permute-start(bf16[2,64,64]{2,1,0:T(8,128)(2,1)} %own_up.1), channel_id=1, source_target_pairs={{0,4},{1,5},{2,6},{3,7},{4,0},{5,1},{6,2},{7,3},{8,12},{9,13},{10,... | collective-permute-start | bytes 49160 | tf_op jit(solution)/shard_map/ppermute | solution.py:580
  4.9 10.1 %collective-permute-start.2 = (bf16[2,2,64,512]{3,2,1,0:T(8,128)(2,1)S(1)}, bf16[2,2,64,512]{3,2,1,0:T(8,128)(2,1)S(1)}, u32[]{:S(2)}, u32[]{:S(2)}) collective-permute-start(bf16[2,2,64,512]{3,2,1,0:T(8,128)(2,1)S(1)} %get-tuple-element.59.refs_8_.refs_2_), channel_id=1, source_target_pairs={{0,8},{1,9},{2,0},{3,1},{4,6},{5,7},{6,14},{7,15},{8,16},{9,17},{1... | collective-permute-start | bytes 786440 | tf_op jit(solution)/shard_map/ppermute | solution.py:604
  8.0 7.0 %collective-permute-start.3 = (bf16[2,64,128]{2,1,0:T(8,128)(2,1)S(1)}, bf16[2,64,128]{2,1,0:T(8,128)(2,1)S(1)}, u32[]{:S(2)}, u32[]{:S(2)}) collective-permute-start(bf16[2,64,128]{2,1,0:T(8,128)(2,1)S(1)} %get-tuple-element.63), channel_id=1, source_target_pairs={{0,0},{16,1},{2,2},{18,3},{6,4},{22,5},{4,6},{20,7},{8,8},{24,9},{... | collective-permute-start | bytes 98312 | tf_op jit(solution)/shard_map/ppermute | solution.py:602
  8.7 6.4 %collective-permute-start.4 = (bf16[2,64,128]{2,1,0:T(8,128)(2,1)S(1)}, bf16[2,64,128]{2,1,0:T(8,128)(2,1)S(1)}, u32[]{:S(2)}, u32[]{:S(2)}) collective-permute-start(bf16[2,64,128]{2,1,0:T(8,128)(2,1)S(1)} %get-tuple-element.63), channel_id=1, source_target_pairs={{8,0},{24,1},{10,2},{26,3},{14,4},{30,5},{12,6},{28,7},{0,8},{16,9... | collective-permute-start | bytes 98312 | tf_op jit(solution)/shard_map/ppermute | solution.py:602
  10.0 8.7 %copy-start.8 = (bf16[4,8,4096]{2,1,0:T(8,128)(2,1)S(1)}, bf16[4,8,4096]{2,1,0:T(8,128)(2,1)}, u32[]{:S(2)}) copy-start(bf16[4,8,4096]{2,1,0:T(8,128)(2,1)} %param.8) | copy-start | bytes 786436
  15.1 11.9 %collective-permute-start.5 = (bf16[2,2,64,512]{3,2,1,0:T(8,128)(2,1)S(1)}, bf16[2,2,64,512]{3,2,1,0:T(8,128)(2,1)S(1)}, u32[]{:S(2)}, u32[]{:S(2)}) collective-permute-start(bf16[2,2,64,512]{3,2,1,0:T(8,128)(2,1)S(1)} %collective-permute-done.2.refs_3_), channel_id=1, source_target_pairs={{0,8},{1,9},{2,0},{3,1},{4,6},{5,7},{6,14},{7,15},{8,16},{9,17},{1... | collective-permute-start | bytes 786440 | tf_op jit(solution)/shard_map/ppermute | solution.py:608
  15.2 11.9 %collective-permute-start.6 = (bf16[2,2,64,512]{3,2,1,0:T(8,128)(2,1)S(1)}, bf16[2,2,64,512]{3,2,1,0:T(8,128)(2,1)S(1)}, u32[]{:S(2)}, u32[]{:S(2)}) collective-permute-start(bf16[2,2,64,512]{3,2,1,0:T(8,128)(2,1)S(1)} %collective-permute-done.2.refs_3_), channel_id=1, source_target_pairs={{0,4},{1,5},{2,6},{3,7},{4,0},{5,1},{6,2},{7,3},{8,12},{9,13},{10,... | collective-permute-start | bytes 786440 | tf_op jit(solution)/shard_map/ppermute | solution.py:609
  18.7 10.7 %collective-permute-start.9 = (bf16[32,4096]{1,0:T(8,128)(2,1)S(1)}, bf16[32,4096]{1,0:T(8,128)(2,1)S(1)}, u32[]{:S(2)}, u32[]{:S(2)}) collective-permute-start(bf16[32,4096]{1,0:T(8,128)(2,1)S(1)} %bitcast.4), channel_id=1, source_target_pairs={{1,0},{0,1},{3,2},{2,3},{5,4},{4,5},{7,6},{6,7},{9,8},{8,9},{11,10... | collective-permute-start | bytes 786440 | tf_op jit(solution)/shard_map/ppermute | solution.py:611
  22.9 4.2 %collective-permute-start.7 = (bf16[2,64,128]{2,1,0:T(8,128)(2,1)S(1)}, bf16[2,64,128]{2,1,0:T(8,128)(2,1)S(1)}, u32[]{:S(2)}, u32[]{:S(2)}) collective-permute-start(bf16[2,64,128]{2,1,0:T(8,128)(2,1)S(1)} %collective-permute-done.3.refs_7_), channel_id=1, source_target_pairs={{0,4},{1,5},{2,6},{3,7},{4,0},{5,1},{6,2},{7,3},{8,12},{9,13},{10,... | collective-permute-start | bytes 98312 | tf_op jit(solution)/shard_map/ppermute | solution.py:610
  22.9 4.2 %collective-permute-start.8 = (bf16[2,64,128]{2,1,0:T(8,128)(2,1)S(1)}, bf16[2,64,128]{2,1,0:T(8,128)(2,1)S(1)}, u32[]{:S(2)}, u32[]{:S(2)}) collective-permute-start(bf16[2,64,128]{2,1,0:T(8,128)(2,1)S(1)} %collective-permute-done.4.refs_8_), channel_id=1, source_target_pairs={{0,4},{1,5},{2,6},{3,7},{4,0},{5,1},{6,2},{7,3},{8,12},{9,13},{10,... | collective-permute-start | bytes 98312 | tf_op jit(solution)/shard_map/ppermute | solution.py:610
  29.3 11.8 %collective-permute-start.10 = (bf16[2,2,64,512]{3,2,1,0:T(8,128)(2,1)S(1)}, bf16[2,2,64,512]{3,2,1,0:T(8,128)(2,1)S(1)}, u32[]{:S(2)}, u32[]{:S(2)}) collective-permute-start(bf16[2,2,64,512]{3,2,1,0:T(8,128)(2,1)S(1)} %collective-permute-done.5.refs_2_), channel_id=1, source_target_pairs={{0,8},{1,9},{2,0},{3,1},{4,6},{5,7},{6,14},{7,15},{8,16},{9,17},{1... | collective-permute-start | bytes 786440 | tf_op jit(solution)/shard_map/ppermute | solution.py:624
  30.2 10.9 %collective-permute-start.11 = (bf16[2,2,64,512]{3,2,1,0:T(8,128)(2,1)S(1)}, bf16[2,2,64,512]{3,2,1,0:T(8,128)(2,1)S(1)}, u32[]{:S(2)}, u32[]{:S(2)}) collective-permute-start(bf16[2,2,64,512]{3,2,1,0:T(8,128)(2,1)S(1)} %collective-permute-done.5.refs_2_), channel_id=1, source_target_pairs={{0,4},{1,5},{2,6},{3,7},{4,0},{5,1},{6,2},{7,3},{8,12},{9,13},{10,... | collective-permute-start | bytes 786440 | tf_op jit(solution)/shard_map/ppermute | solution.py:628
  34.6 3.3 %copy-start = (bf16[8192,512]{1,0:T(8,128)(2,1)}, bf16[8192,512]{1,0:T(8,128)(2,1)S(1)}, u32[]{:S(2)}) copy-start(bf16[8192,512]{1,0:T(8,128)(2,1)S(1)} %get-tuple-element.78.refs_0_) | copy-start | bytes 25165828
  37.9 3.2 %copy-start.4 = (bf16[8192,512]{1,0:T(8,128)(2,1)}, bf16[8192,512]{1,0:T(8,128)(2,1)S(1)}, u32[]{:S(2)}) copy-start(bf16[8192,512]{1,0:T(8,128)(2,1)S(1)} %get-tuple-element.79.refs_1_) | copy-start | bytes 25165828
  41.1 12.8 %collective-permute-start.13 = (bf16[2,2,64,512]{3,2,1,0:T(8,128)(2,1)S(1)}, bf16[2,2,64,512]{3,2,1,0:T(8,128)(2,1)S(1)}, u32[]{:S(2)}, u32[]{:S(2)}) collective-permute-start(bf16[2,2,64,512]{3,2,1,0:T(8,128)(2,1)S(1)} %collective-permute-done.10.refs_2_), channel_id=1, source_target_pairs={{0,4},{1,5},{2,6},{3,7},{4,0},{5,1},{6,2},{7,3},{8,12},{9,13},{10,... | collective-permute-start | bytes 786440 | tf_op jit(solution)/shard_map/ppermute | solution.py:628
  41.6 12.2 %collective-permute-start.12 = (bf16[1,2,64,512]{3,2,1,0:T(8,128)(2,1)S(1)}, bf16[1,2,64,512]{3,2,1,0:T(8,128)(2,1)S(1)}, u32[]{:S(2)}, u32[]{:S(2)}) collective-permute-start(bf16[1,2,64,512]{3,2,1,0:T(8,128)(2,1)S(1)} %constant_dynamic-slice_fusion), channel_id=1, source_target_pairs={{0,8},{1,9},{2,0},{3,1},{4,6},{5,7},{6,14},{7,15},{8,16},{9,17},{1... | collective-permute-start | bytes 393224 | tf_op jit(solution)/shard_map/ppermute | solution.py:627
  44.0 3.4 %copy-start.1 = (bf16[8192,512]{1,0:T(8,128)(2,1)S(1)}, bf16[8192,512]{1,0:T(8,128)(2,1)}, u32[]{:S(2)}) copy-start(bf16[8192,512]{1,0:T(8,128)(2,1)} %copy-done) | copy-start | bytes 25165828
  47.4 3.4 %copy-start.5 = (bf16[8192,512]{1,0:T(8,128)(2,1)S(1)}, bf16[8192,512]{1,0:T(8,128)(2,1)}, u32[]{:S(2)}) copy-start(bf16[8192,512]{1,0:T(8,128)(2,1)} %copy-done.4) | copy-start | bytes 25165828
  53.9 10.3 %collective-permute-start.14 = (bf16[1,2,64,512]{3,2,1,0:T(8,128)(2,1)S(1)}, bf16[1,2,64,512]{3,2,1,0:T(8,128)(2,1)S(1)}, u32[]{:S(2)}, u32[]{:S(2)}) collective-permute-start(bf16[1,2,64,512]{3,2,1,0:T(8,128)(2,1)S(1)} %collective-permute-done.12.refs_4_), channel_id=1, source_target_pairs={{0,4},{1,5},{2,6},{3,7},{4,0},{5,1},{6,2},{7,3},{8,12},{9,13},{10,... | collective-permute-start | bytes 393224 | tf_op jit(solution)/shard_map/ppermute | solution.py:633
  57.7 3.3 %copy-start.2 = (bf16[8192,512]{1,0:T(8,128)(2,1)}, bf16[8192,512]{1,0:T(8,128)(2,1)S(1)}, u32[]{:S(2)}) copy-start(bf16[8192,512]{1,0:T(8,128)(2,1)S(1)} %get-tuple-element.97.refs_0_) | copy-start | bytes 25165828
  60.9 3.2 %copy-start.6 = (bf16[8192,512]{1,0:T(8,128)(2,1)}, bf16[8192,512]{1,0:T(8,128)(2,1)S(1)}, u32[]{:S(2)}) copy-start(bf16[8192,512]{1,0:T(8,128)(2,1)S(1)} %get-tuple-element.98.refs_1_) | copy-start | bytes 25165828
  64.2 3.4 %copy-start.3 = (bf16[8192,512]{1,0:T(8,128)(2,1)S(1)}, bf16[8192,512]{1,0:T(8,128)(2,1)}, u32[]{:S(2)}) copy-start(bf16[8192,512]{1,0:T(8,128)(2,1)} %copy-done.2) | copy-start | bytes 25165828
  67.5 3.4 %copy-start.7 = (bf16[8192,512]{1,0:T(8,128)(2,1)S(1)}, bf16[8192,512]{1,0:T(8,128)(2,1)}, u32[]{:S(2)}) copy-start(bf16[8192,512]{1,0:T(8,128)(2,1)} %copy-done.6) | copy-start | bytes 25165828
where the time goes:
time: 74.8 us; the launch traced here: 74.4 us
  Pallas kernels  26.9 us (36%)
  local copies, waits for them, and re-layouts  26.5 us (35%)
  starting transfers between devices  17.7 us (24%)
  waiting for transfers between devices  2.31 us (3%)
  between operations  1.01 us (1%)
    unnamed x20, local copies, waits for them, and re-layouts  26.5 us
    pallas_call x4, Pallas kernels, merge(): pl.pallas_call(functools.partial(merge_blocks, lay, [e[:3] for e in entri...  14.5 us
    pallas_call x2, Pallas kernels, cache_attention(): pl.pallas_call(functools.partial(attend_cache, part, pairs, sizes, scale,...  8.73 us
    ppermute x1, starting transfers between devices, shards(): hidden = [send(tokens, perm=lay.feature_step(i)) for i in range(1, lay.tp)]  4.18 us
    ppermute x4, starting transfers between devices, shards(): swapped = send(came, perm=swap)  4.1 us
    ppermute x1, starting transfers between devices, shards(): came = send(pair, perm=ring)  3.11 us
    pallas_call x1, Pallas kernels, begin(): pl.pallas_call(functools.partial(begin_blocks, sizes, kv), out_shape=(plt...  2.72 us
    ppermute x1, starting transfers between devices, shards(): sent = send(lax.dynamic_slice_in_dim(came, core, 1, 0), perm=ring)  2.36 us
  transfers between devices with their start and end apart: 15, of which 1 were waited for; matrix products, arithmetic and copies ran while one was open for 0% of the time, Pallas kernels for 30%

commit v1 on v0

--- a/solution.py
+++ b/solution.py
@@ -60,17 +60,34 @@
             for z, c, g, t in self.devices()
         ]
 
-    def column_step(self, turn):
+    def sources(self, t):
+        count = self.block * self.grp
+        places = sorted(
+            self.place(z, g)
+            for z in range(t * self.block, (t + 1) * self.block)
+            for g in range(self.grp)
+        )
+        assert sorted(p % count for p in places) == list(range(count)) and count <= 4
+        return sorted(places, key=lambda p: p % count)
+
+    def column_step(self, flip):
+        count = self.block * self.grp
         pairs = []
-        for z, c, g, t in self.devices():
-            shift, turn_g = divmod(2 * turn + c, self.grp)
-            source = t * self.block + (z % self.block + shift) % self.block
-            pairs.append(
-                (
-                    self.flat(source, c, (g + turn_g) % self.grp, z // self.block),
-                    self.flat(z, c, g, t),
-                )
-            )
+        for t in range(self.tp):
+            for s, source in enumerate(self.sources(t)):
+                places = list(range(s, self.ring, count))
+                places.remove(source)
+                others = [x for x in range(self.tp) if x != t]
+                for to, lane in [(source, t)] + list(zip(places, others)):
+                    for c in range(2):
+                        from_z, from_g = self.at(source)
+                        to_z, to_g = self.at(to)
+                        pairs.append(
+                            (
+                                self.flat(from_z, c ^ flip, from_g, lane),
+                                self.flat(to_z, c, to_g, t),
+                            )
+                        )
         return pairs
 
 
@@ -171,35 +188,30 @@
     )(pinned(lengths), pinned(queries), pinned(keys), pinned(values))
 
 
-def pack_pair(own_hbm, other, own_up, other_up, *refs):
-    pair, up_pair, sems = refs[-3:]
-    core = lax.rem(lax.axis_index("fsdp"), 2)
-    copies = [
-        pltpu.make_async_copy(own_hbm, pair.at[core], sems.at[0]),
-        pltpu.make_async_copy(other, pair.at[1 - core], sems.at[1]),
-    ]
-    for copy in copies:
-        copy.start()
-    for ref, place in ((own_up, core), (other_up, 1 - core)):
-        up_pair[place] = jnp.concatenate([ref[k] for k in range(ref.shape[0])], axis=1)
-    for copy in copies:
-        copy.wait()
+def pack_pair(own, other, own_up, other_up, *refs):
+    pair = refs[-1]
+    lanes = pair.shape[3]
+    for place, (down, up) in enumerate(((own, own_up), (other, other_up))):
+        count, _, depth = down.shape
+        tiles = depth // lanes
+        for k in range(count):
+            for i in range(tiles):
+                pair[place, k * tiles + i] = down[k, :, i * lanes : (i + 1) * lanes]
+        columns = jnp.concatenate([up[k] for k in range(count)], axis=1)
+        pair[place, count * tiles, :, : columns.shape[1]] = columns
 
 
 def pack(own, other, own_up, other_up, after):
-    count, rank, columns = own_up.shape
+    count, rank, depth = own.shape
+    tiles = count * depth // 128 + 1
     return pl.pallas_call(
         pack_pair,
-        out_shape=(
-            pltpu.VMEM((2,) + own.shape, own.dtype),
-            pltpu.VMEM((2, rank, count * columns), own.dtype),
-        ),
-        in_specs=[HBM, ANY, VMEM, VMEM] + [ANY] * len(after),
-        out_specs=(VMEM, VMEM),
-        scratch_shapes=[pltpu.SemaphoreType.DMA((2,))],
+        out_shape=pltpu.VMEM((2, tiles, rank, 128), own.dtype),
+        in_specs=[VMEM] * 4 + [ANY] * len(after),
+        out_specs=VMEM,
         compiler_params=pltpu.CompilerParams(vmem_limit_bytes=4 * MIB),
         name="pack_pair",
-    )(pinned(own), other, own_up, other_up, *after)
+    )(own, other, own_up, other_up, *after)
 
 
 def attend_cache(part, pairs, sizes, scale, n_kept, *refs):
@@ -360,22 +372,34 @@
 
     pairs, depth, width = m_buf.shape[1:]
     cut = min(width, 256)
+    lanes = downs[0].shape[3]
+    tiles = depth // lanes
     fsdp, grp, tp = (lax.axis_index(a) for a in AXES)
     z, core = fsdp // 2, lax.rem(fsdp, 2)
     place = grp * lay.depth + jnp.where(lax.rem(grp, 2) == 0, z, lay.depth - 1 - z)
     per_lane = lay.fsdp * lay.grp // lay.tp
 
+    def position(step, flip):
+        towards = 2 * core - 1
+        return lax.rem(place + lay.ring + step * (-towards if flip else towards), lay.ring)
+
     if first:
         for i, h in enumerate(hidden):
             h_buf[lax.rem(tp + i, lay.tp)] = h[...]
-        for i, up in enumerate(ups):
-            flip, turn = divmod(i, len(ups) // 2)
-            spot = 2 * turn + (1 - core if flip else core)
-            shift, turn = spot // lay.grp, lax.rem(spot, lay.grp)
-            zz = lax.rem(lax.rem(z, lay.block) + shift, lay.block)
+        columns = width // u_parts.shape[0]
+        tables = [lay.sources(t) for t in range(lay.tp)]
+        for (step, flip), up in zip([e[:2] for e in plan] + [(2, False)], downs + ups):
+            remainder = lax.rem(position(step, flip), len(tables[0]))
+            source = jnp.int32(0)
+            for t, table in enumerate(tables):
+                for i, spot in enumerate(table):
+                    source = jnp.where((tp == t) & (remainder == i), spot, source)
+            g = source // lay.depth
+            along = lax.rem(source, lay.depth)
+            zz = jnp.where(lax.rem(g, 2) == 0, along, lay.depth - 1 - along) - tp * lay.block
             for c in range(2):
-                u_parts[(zz * 2 + c) * lay.grp + lax.rem(grp + turn, lay.grp)] = up[c]
-        columns = u_parts.shape[2] // pairs
+                cc = lax.rem(core + c + (1 if flip else 0), 2)
+                u_parts[(zz * 2 + cc) * lay.grp + g] = up[c, pairs * tiles, :, : pairs * columns]
         for k in range(pairs):
             u_buf[k] = ADAPTER_SCALING * jnp.concatenate(
                 [u_parts[i, :, k * columns : (k + 1) * columns] for i in range(u_parts.shape[0])],
@@ -389,14 +413,14 @@
 
     chunk = min(depth, 256)
     j = 0
-    for (step, flip, whole), down in zip(plan, downs):
-        towards = 2 * core - 1
-        spot = lax.rem(place + lay.ring + step * (-towards if flip else towards), lay.ring)
+    for (step, flip), down in zip(plan, downs):
+        spot = position(step, flip)
         g = spot // lay.depth
         along = lax.rem(spot, lay.depth)
         zz = jnp.where(lax.rem(g, 2) == 0, along, lay.depth - 1 - along)
-        def block(c, j=j, down=down, flip=flip, whole=whole, zz=zz):
-            cc = c if whole else (1 - core if flip else core)
+
+        def block(c, j=j, down=down, flip=flip, zz=zz, g=g):
+            cc = lax.rem(core + c + (1 if flip else 0), 2)
             index = (zz * 2 + cc) * lay.grp + g
             start = pl.multiple_of(index * depth, depth)
             column = pl.multiple_of(lax.rem(index, per_lane) * depth, depth)
@@ -404,7 +428,10 @@
             for k in range(pairs):
                 for begin in range(0, depth, chunk):
                     rows = slice(begin, begin + chunk)
-                    d = down[c, k, :, rows]
+                    tile = k * tiles + begin // lanes
+                    d = jnp.concatenate(
+                        [down[c, tile + i] for i in range(chunk // lanes)], axis=1
+                    )
                     h = h_buf[source, :, pl.ds(column + begin, chunk)]
                     for side in range(width // cut):
                         cols = slice(side * cut, (side + 1) * cut)
@@ -426,11 +453,8 @@
                     m_buf.at[j + c, k], m_hbm.at[k, pl.ds(start, depth), :], sems.at[j + c, k]
                 ).start()
 
-        if down.shape[0] == 1:
-            block(0)
-        else:
-            pl.loop(0, down.shape[0])(block)
-        j += down.shape[0]
+        pl.loop(0, 2)(block)
+        j += 2
 
     if last:
         new = []
@@ -486,10 +510,11 @@
 
 def merge(lay, shape, entries, weights, inputs, state, final, after):
     pairs, total, width = shape
-    rank, depth = entries[0][3].shape[2:]
+    rank = entries[0][2].shape[2]
+    depth = total // (lay.fsdp * lay.grp)
     first, last = state is None, final is not None
-    n = sum(e[3].shape[0] for e in entries)
-    operands = [pinned(w, pltpu.VMEM) for w in weights] + [e[3] for e in entries]
+    n = 2 * len(entries)
+    operands = [pinned(w, pltpu.VMEM) for w in weights] + [e[2] for e in entries]
     specs = [VMEM] * len(operands)
     counts = (0, 0)
     aliases = {0: 1, 1: 2}
@@ -518,8 +543,8 @@
             pltpu.VMEM(s, jnp.bfloat16)
             for s in ((pairs, rank, width), (lay.tp, tokens, features))
         ]
-        parts = len(ups) * 2
-        scratch.append(pltpu.VMEM((parts,) + ups[0].shape[1:], jnp.bfloat16))
+        parts = 2 * lay.block * lay.grp
+        scratch.append(pltpu.VMEM((parts, rank, pairs * width // parts), jnp.bfloat16))
     if last:
         order, queries, caches = final
         operands += [pinned(order, pltpu.SMEM), pinned(queries, pltpu.VMEM)] + caches
@@ -533,7 +558,7 @@
     specs += [ANY] * len(after)
     out = pl.pallas_call(
         functools.partial(
-            merge_blocks, lay, [e[:3] for e in entries], counts, first, last, scale
+            merge_blocks, lay, [e[:2] for e in entries], counts, first, last, scale
         ),
         out_shape=out_shape,
         in_specs=specs,
@@ -577,9 +602,10 @@
     swap, ring = lay.core_swap(), lay.ring_step()
     caches = []
 
-    other, other_up = send(own, perm=swap), send(factor_up, perm=swap)
+    other = send(own, perm=swap)
+    own_up, other_up = (send(factor_up, perm=lay.column_step(flip)) for flip in range(2))
     lengths, order, q, *buffers = begin(cache_lengths, queries, keys, values, sizes, kv)
-    pair, up_pair = pack(own, other, factor_up, other_up, [q])
+    pair = pack(own, other, own_up, other_up, [q])
 
     def attention(part, buffers, kept, after):
         out = cache_attention(
@@ -598,42 +624,29 @@
         caches.extend(out[3:5])
         return out[:2], [*out[5:], out[2]]
 
-    ups = [
-        send(up_pair, perm=lay.column_step(turn)) for turn in range(lay.block * lay.grp // 2)
-    ]
     came = send(pair, perm=ring)
     buffers, weights = attention(0, buffers, [], [pair])
-    (came, ups, tokens), token = after_all((came, ups, tokens), caches[0])
+    (came, tokens), token = after_all((came, tokens), caches[0])
 
     sent = send(came, perm=ring)
     swapped = send(came, perm=swap)
-    other_ups = [send(u, perm=swap) for u in ups]
     hidden = [send(tokens, perm=lay.feature_step(i)) for i in range(1, lay.tp)]
     buffers, weights = attention(1, buffers, weights, [token])
-    (sent, swapped, other_ups, hidden), token = after_all(
-        (sent, swapped, other_ups, hidden), caches[2]
-    )
-    entries = [(0, False, True, pair), (1, False, True, came), (1, True, True, swapped)]
+    (sent, swapped, hidden), token = after_all((sent, swapped, hidden), caches[2])
+    entries = [(0, False, pair), (1, False, came), (1, True, swapped)]
     came = sent
 
-    inputs = ([tokens] + hidden, ups + other_ups)
+    inputs = ([tokens] + hidden, [came])
     state = None
     last_step = lay.ring // 2
     for step in range(2, last_step):
-        if step + 1 < last_step:
-            sent = send(came, perm=ring)
-        else:
-            core = lax.rem(lax.axis_index("fsdp"), 2)
-            sent = send(lax.dynamic_slice_in_dim(came, core, 1, 0), perm=ring)
+        sent = send(came, perm=ring)
         swapped = send(came, perm=swap)
         state, weights = merge(lay, shape, entries, weights, inputs, state, None, [token])
         (sent, swapped), token = after_all((sent, swapped), state[3])
-        entries = [(step, False, True, came), (step, True, True, swapped)]
+        entries = [(step, False, came), (step, True, swapped)]
         came = sent
-    swapped = send(came, perm=swap)
-    entries.append((last_step, False, False, came))
-    state, weights = merge(lay, shape, entries, weights, inputs, state, None, [token])
-    entries = [(last_step, True, False, swapped)]
+    entries.append((last_step, False, came))
     out, _ = merge(lay, shape, entries, weights, inputs, state, (order, q, caches), [])
     return tuple(out)
 

time: 74.8 us -> 52.2 us (0.70)
  local copies, waits for them, and re-layouts: 26.5 us -> 0.01 us
  waiting for transfers between devices: 2.31 us -> 5.93 us
    unnamed x20 -> x4, local copies, waits for them, and re-layouts: 26.5 us -> 0.01 us
    ppermute x2 -> x3, starting transfers between devices: 0.91 us -> 8.6 us  [shards(): sent = send(came, perm=ring)]
    ppermute x4 -> x3, starting transfers between devices: 4.1 us -> 0.19 us  [shards(): swapped = send(came, perm=swap)]
    ppermute x7 -> x3, starting transfers between devices: 5.37 us -> 2 us  [the longest x2 1.48 us: shards(): send(factor_up, perm=lay.column_step(flip))]
    ppermute x2 -> x3, waiting for transfers between devices: 0.01 us -> 3.07 us  [shards(): sent = send(came, perm=ring)]
    pallas_call x5 -> x4, Pallas kernels: 15.5 us -> 14 us  [the longest x3 13.9 us: merge(): pl.pallas_call(functools.partial(merge_blocks, lay, [e[:2] for e in entri...]
    pallas_call x2, Pallas kernels: 8.73 us -> 10.1 us  [cache_attention(): pl.pallas_call(functools.partial(attend_cache, part, pairs, sizes, scale,...]
  transfers between devices with their start and end apart: 15 -> 11, of which waited for: 1 -> 3; matrix products, arithmetic and copies ran while one was open for 0% -> 0% of each run, Pallas kernels for 30% -> 39%
where the time goes in v1:
time: 52.2 us; the launch traced here: 52 us
  Pallas kernels  26.7 us (51%)
  starting transfers between devices  18.4 us (35%)
  waiting for transfers between devices  5.93 us (11%)
  between operations  0.91 us (2%)
    pallas_call x3, Pallas kernels, merge(): pl.pallas_call(functools.partial(merge_blocks, lay, [e[:2] for e in entri...  13.9 us
    pallas_call x2, Pallas kernels, cache_attention(): pl.pallas_call(functools.partial(attend_cache, part, pairs, sizes, scale,...  10.1 us
    ppermute x3, starting transfers between devices, shards(): sent = send(came, perm=ring)  8.6 us
    ppermute x1, starting transfers between devices, shards(): hidden = [send(tokens, perm=lay.feature_step(i)) for i in range(1, lay.tp)]  4.88 us
    ppermute x3, waiting for transfers between devices, shards(): sent = send(came, perm=ring)  3.07 us
    ppermute x1, waiting for transfers between devices, shards(): hidden = [send(tokens, perm=lay.feature_step(i)) for i in range(1, lay.tp)]  2.85 us
    pallas_call x1, Pallas kernels, begin(): pl.pallas_call(functools.partial(begin_blocks, sizes, kv), out_shape=(plt...  2.72 us
    ppermute x1, starting transfers between devices, shards(): came = send(pair, perm=ring)  2.7 us
  transfers between devices with their start and end apart: 11, of which 3 were waited for; matrix products, arithmetic and copies ran while one was open for 0% of the time, Pallas kernels for 39%

profile of v1, /device:TPU:0, one launch (start us, length us, event | category | flops | bytes accessed | tf_op | source)
XLA Modules:
  0.0 52.0 jit_solution(9121186878683355810)
XLA Ops:
  0.6 0.0 copy-start.1
  0.6 0.5 collective-permute-start
  1.2 0.1 collective-permute-start.2
  1.2 1.4 %collective-permute-start.1 = (bf16[2,64,64]{2,1,0:T(8,128)(2,1)}, bf16[2,64,64]{2,1,0:T(8,128)(2,1)S(1)}, u32[]{:S(2)}, u32[]{:S(2)}) collective-permute-start(bf16[2,64,64]{2,1,0:T(8,128)(2,1)} %param.15), channel_id=1, source_target_pairs={{0,0},{4,4},{1,26},{5,30},{8,8},{12,12},{9,18},{13,22},{10,10},{14... | collective-permute-start | bytes 49160 | tf_op jit(solution)/shard_map/ppermute | solution.py:606
  2.6 2.7 %begin.1 = (s32[8]{0:T(128)S(4)}, s32[8]{0:T(128)S(4)}, bf16[4,8,32,128]{3,2,1,0:T(8,128)(2,1)S(1)}, bf16[4,3072,128]{2,1,0:T(8,128)(2,1)S(1)}, bf16[4,3072,128]{2,1,0:T(8,128)(2,1)S(1)}) custom-call(s32[8]{0:T(128)} %len_hbm.1, bf16[4,8,32,128]{3,2,1,0:T(8,128)(2,1)} %q_hbm.1, bf16[8,3072,128]{2,1,0:T(8,128)(2,1)} %bitcast.8, bf16[8,3072,128]{2,1,0:T(8,128)(2,1)} %bitcast.11), custom_call_target="tpu_custom_call" | custom-call | bytes 3145728 | tf_op jit(solution)/shard_map/begin/pallas_call | solution.py:171
  5.4 0.0 collective-permute-done.2.other_up
  5.4 0.0 collective-permute-done.1.own_up
  5.4 0.0 collective-permute-done.other
  5.4 0.0 copy-done.1
  5.4 0.1 pack_pair.1.refs_8_.refs_2_
  5.5 2.7 %collective-permute-start.3 = (bf16[2,9,64,128]{3,2,1,0:T(8,128)(2,1)S(1)}, bf16[2,9,64,128]{3,2,1,0:T(8,128)(2,1)S(1)}, u32[]{:S(2)}, u32[]{:S(2)}) collective-permute-start(bf16[2,9,64,128]{3,2,1,0:T(8,128)(2,1)S(1)} %pack_pair.1.refs_8_.refs_2_), channel_id=1, source_target_pairs={{0,8},{1,9},{2,0},{3,1},{4,6},{5,7},{6,14},{7,15},{8,16},{9,17},{1... | collective-permute-start | bytes 884744 | tf_op jit(solution)/shard_map/ppermute | solution.py:627
  8.2 0.0 copy-start
  8.2 5.8 %cache_attention.2 = (bf16[4,3072,128]{2,1,0:T(8,128)(2,1)S(1)}, bf16[4,3072,128]{2,1,0:T(8,128)(2,1)S(1)}, bf16[8192,512]{1,0:T(8,128)(2,1)S(1)}, f32[4,128,128]{2,1,0:T(8,128)S(1)}, f32[4,128,128]{2,1,0:T(8,128)S(1)}) custom-call(s32[8]{0:T(128)S(4)} %get-tuple-element.42.refs_0_, ...), custom_call_target="tpu_custom_call", output_to_operand_aliasing={{0}: (6, {}), {1}: (7, {})} | custom-call | flops 805306368 | bytes 14680064 | tf_op jit(solution)/shard_map/cache_attention/pallas_call | solution.py:314
  14.0 0.0 collective-permute-done.3.refs_3_
  14.1 0.1 collective-permute-start.5
  14.1 5.8 %collective-permute-start.4 = (bf16[2,9,64,128]{3,2,1,0:T(8,128)(2,1)S(1)}, bf16[2,9,64,128]{3,2,1,0:T(8,128)(2,1)S(1)}, u32[]{:S(2)}, u32[]{:S(2)}) collective-permute-start(bf16[2,9,64,128]{3,2,1,0:T(8,128)(2,1)S(1)} %collective-permute-done.3.refs_3_), channel_id=1, source_target_pairs={{0,8},{1,9},{2,0},{3,1},{4,6},{5,7},{6,14},{7,15},{8,16},{9,17},{1... | collective-permute-start | bytes 884744 | tf_op jit(solution)/shard_map/ppermute | solution.py:631
  19.9 0.0 copy-done
  19.9 4.9 %collective-permute-start.6 = (bf16[32,4096]{1,0:T(8,128)(2,1)S(1)}, bf16[32,4096]{1,0:T(8,128)(2,1)S(1)}, u32[]{:S(2)}, u32[]{:S(2)}) collective-permute-start(bf16[32,4096]{1,0:T(8,128)(2,1)S(1)} %bitcast.4), channel_id=1, source_target_pairs={{1,0},{0,1},{3,2},{2,3},{5,4},{4,5},{7,6},{6,7},{9,8},{8,9},{11,10... | collective-permute-start | bytes 786440 | tf_op jit(solution)/shard_map/ppermute | solution.py:633
  24.8 4.2 %cache_attention.3 = (bf16[4,3072,128]{2,1,0:T(8,128)(2,1)S(1)}, bf16[4,3072,128]{2,1,0:T(8,128)(2,1)S(1)}, bf16[8192,512]{1,0:T(8,128)(2,1)S(1)}, f32[4,128,128...) custom-call(s32[8]{0:T(128)S(4)} %get-tuple-element.42.refs_0_, ...), custom_call_target="tpu_custom_call", output_to_operand_aliasing={{0}: (6, {}), {1}: (7, {}), {5}: (8, {})} | custom-call | flops 805306368 | bytes 14680064 | tf_op jit(solution)/shard_map/cache_attention/pallas_call | solution.py:314
  29.1 2.8 %collective-permute-done.6.refs_6_ = bf16[32,4096]{1,0:T(8,128)(2,1)S(1)} collective-permute-done((bf16[32,4096]{1,0:T(8,128)(2,1)S(1)}, bf16[32,4096]{1,0:T(8,128)(2,1)S(1)}, u32[]{:S(2)}, u32[]{:S(2)}) %collective-permute-start.6) | collective-permute-done | bytes 262176 | tf_op jit(solution)/shard_map/ppermute | solution.py:633
  31.9 0.0 collective-permute-done.5.refs_4_
  31.9 0.0 collective-permute-done.4.refs_7_.refs_2_
  31.9 0.1 collective-permute-start.8
  32.0 1.4 %collective-permute-start.7 = (bf16[2,9,64,128]{3,2,1,0:T(8,128)(2,1)S(1)}, bf16[2,9,64,128]{3,2,1,0:T(8,128)(2,1)S(1)}, u32[]{:S(2)}, u32[]{:S(2)}) collective-permute-start(bf16[2,9,64,128]{3,2,1,0:T(8,128)(2,1)S(1)} %collective-permute-done.4.refs_7_.refs_2_), channel_id=1, source_target_pairs={{0,8},{1,9},{2,0},{3,1},{4,6},{5,7},{6,14},{7,15},{8,16},{9,17},{1... | collective-permute-start | bytes 884744 | tf_op jit(solution)/shard_map/ppermute | solution.py:643
  33.4 4.4 %merge_blocks.3 = (bf16[2,8192,512]{2,1,0:T(8,128)(2,1)}, bf16[8192,512]{1,0:T(8,128)(2,1)S(1)}, bf16[8192,512]{1,0:T(8,128)(2,1)S(1)}, bf16[2,64,512]{2,1,0:T(8...) custom-call(bf16[8192,512]{1,0:T(8,128)(2,1)S(1)} %get-tuple-element, ...), custom_call_target="tpu_custom_call", output_to_operand_aliasing={{1}: (0, {}), {2}: (1, {})} | custom-call | flops 603979776 | bytes 6291456 | tf_op jit(solution)/shard_map/merge_blocks/pallas_call | solution.py:559
  37.9 0.0 collective-permute-done.8.refs_3_
  37.9 0.9 %collective-permute-done.7.refs_2_ = bf16[2,9,64,128]{3,2,1,0:T(8,128)(2,1)S(1)} collective-permute-done((bf16[2,9,64,128]{3,2,1,0:T(8,128)(2,1)S(1)}, bf16[2,9,64,128]{3,2,1,0:T(8,128)(2,1)S(1)}, u32[]{:S(2)}, u32[]{:S(2)}) %collective-permute-start.7) | collective-permute-done | bytes 294944 | tf_op jit(solution)/shard_map/ppermute | solution.py:643
  38.8 0.0 collective-permute-start.10
  38.8 1.4 %collective-permute-start.9 = (bf16[2,9,64,128]{3,2,1,0:T(8,128)(2,1)S(1)}, bf16[2,9,64,128]{3,2,1,0:T(8,128)(2,1)S(1)}, u32[]{:S(2)}, u32[]{:S(2)}) collective-permute-start(bf16[2,9,64,128]{3,2,1,0:T(8,128)(2,1)S(1)} %collective-permute-done.7.refs_2_), channel_id=1, source_target_pairs={{0,8},{1,9},{2,0},{3,1},{4,6},{5,7},{6,14},{7,15},{8,16},{9,17},{1... | collective-permute-start | bytes 884744 | tf_op jit(solution)/shard_map/ppermute | solution.py:643
  40.2 3.1 %merge_blocks.4 = (bf16[2,8192,512]{2,1,0:T(8,128)(2,1)}, bf16[8192,512]{1,0:T(8,128)(2,1)S(1)}, bf16[8192,512]{1,0:T(8,128)(2,1)S(1)}, f32[2,32,512]{2,1,0:T(8,128)S(1)}, f32[2,32,64]{2,1,0:T(8,128)S(1)}) custom-call(bf16[8192,512]{1,0:T(8,128)(2,1)S(1)} %get-tuple-element.61.refs_0_, ...), custom_call_target="tpu_custom_call", output_to_operand_aliasing={{1}: (0, {}), {2}: (1, {}), {0}: (6, {})} | custom-call | flops 402653184 | bytes 4194304 | tf_op jit(solution)/shard_map/merge_blocks/pallas_call | solution.py:559
  43.3 0.0 collective-permute-done.10.refs_3_
  43.3 2.2 %collective-permute-done.9.refs_4_ = bf16[2,9,64,128]{3,2,1,0:T(8,128)(2,1)S(1)} collective-permute-done((bf16[2,9,64,128]{3,2,1,0:T(8,128)(2,1)S(1)}, bf16[2,9,64,128]{3,2,1,0:T(8,128)(2,1)S(1)}, u32[]{:S(2)}, u32[]{:S(2)}) %collective-permute-start.9) | collective-permute-done | bytes 294944 | tf_op jit(solution)/shard_map/ppermute | solution.py:643
  45.5 6.3 %merge_blocks.5 = (bf16[2,8192,512]{2,1,0:T(8,128)(2,1)}, bf16[8192,512]{1,0:T(8,128)(2,1)S(1)}, bf16[8192,512]{1,0:T(8,128)(2,1)S(1)}, bf16[4,8,32,128]{3,2,1,0:T(8,128)(2,1)}) custom-call(bf16[8192,512]{1,0:T(8,128)(2,1)S(1)} %get-tuple-element.70.refs_0_, ...), custom_call_target="tpu_custom_call", output_to_operand_aliasing={{1}: (0, {}), {2}: (1, {}), {0}: (7, {})} | custom-call | flops 603979776 | bytes 6291456 | tf_op jit(solution)/shard_map/merge_blocks/pallas_call | solution.py:559
Async XLA Ops:
  0.6 4.8 %copy-start.1 = (bf16[2,512,64]{1,2,0:T(8,128)(2,1)S(1)}, bf16[2,512,64]{1,2,0:T(8,128)(2,1)}, u32[]{:S(2)}) copy-start(bf16[2,512,64]{1,2,0:T(8,128)(2,1)} %param.14) | copy-start | bytes 393220
  0.6 4.7 %collective-permute-start = (bf16[2,64,512]{2,1,0:T(8,128)(2,1)}, bf16[2,64,512]{2,1,0:T(8,128)(2,1)S(1)}, u32[]{:S(2)}, u32[]{:S(2)}) collective-permute-start(bf16[2,64,512]{2,1,0:T(8,128)(2,1)} %bitcast.6), channel_id=1, source_target_pairs={{0,4},{1,5},{2,6},{3,7},{4,0},{5,1},{6,2},{7,3},{8,12},{9,13},{10,... | collective-permute-start | bytes 393224 | tf_op jit(solution)/shard_map/ppermute | solution.py:605
  1.2 4.2 %collective-permute-start.2 = (bf16[2,64,64]{2,1,0:T(8,128)(2,1)}, bf16[2,64,64]{2,1,0:T(8,128)(2,1)S(1)}, u32[]{:S(2)}, u32[]{:S(2)}) collective-permute-start(bf16[2,64,64]{2,1,0:T(8,128)(2,1)} %param.15), channel_id=1, source_target_pairs={{4,0},{0,4},{5,26},{1,30},{12,8},{8,12},{13,18},{9,22},{14,10},{10... | collective-permute-start | bytes 49160 | tf_op jit(solution)/shard_map/ppermute | solution.py:606
  1.2 4.1 %collective-permute-start.1 = (bf16[2,64,64]{2,1,0:T(8,128)(2,1)}, bf16[2,64,64]{2,1,0:T(8,128)(2,1)S(1)}, u32[]{:S(2)}, u32[]{:S(2)}) collective-permute-start(bf16[2,64,64]{2,1,0:T(8,128)(2,1)} %param.15), channel_id=1, source_target_pairs={{0,0},{4,4},{1,26},{5,30},{8,8},{12,12},{9,18},{13,22},{10,10},{14... | collective-permute-start | bytes 49160 | tf_op jit(solution)/shard_map/ppermute | solution.py:606
  5.5 8.6 %collective-permute-start.3 = (bf16[2,9,64,128]{3,2,1,0:T(8,128)(2,1)S(1)}, bf16[2,9,64,128]{3,2,1,0:T(8,128)(2,1)S(1)}, u32[]{:S(2)}, u32[]{:S(2)}) collective-permute-start(bf16[2,9,64,128]{3,2,1,0:T(8,128)(2,1)S(1)} %pack_pair.1.refs_8_.refs_2_), channel_id=1, source_target_pairs={{0,8},{1,9},{2,0},{3,1},{4,6},{5,7},{6,14},{7,15},{8,16},{9,17},{1... | collective-permute-start | bytes 884744 | tf_op jit(solution)/shard_map/ppermute | solution.py:627
  8.2 11.8 %copy-start = (bf16[4,8,4096]{2,1,0:T(8,128)(2,1)S(1)}, bf16[4,8,4096]{2,1,0:T(8,128)(2,1)}, u32[]{:S(2)}) copy-start(bf16[4,8,4096]{2,1,0:T(8,128)(2,1)} %param.8) | copy-start | bytes 786436
  14.1 17.9 %collective-permute-start.5 = (bf16[2,9,64,128]{3,2,1,0:T(8,128)(2,1)S(1)}, bf16[2,9,64,128]{3,2,1,0:T(8,128)(2,1)S(1)}, u32[]{:S(2)}, u32[]{:S(2)}) collective-permute-start(bf16[2,9,64,128]{3,2,1,0:T(8,128)(2,1)S(1)} %collective-permute-done.3.refs_3_), channel_id=1, source_target_pairs={{0,4},{1,5},{2,6},{3,7},{4,0},{5,1},{6,2},{7,3},{8,12},{9,13},{10,... | collective-permute-start | bytes 884744 | tf_op jit(solution)/shard_map/ppermute | solution.py:632
  14.1 17.8 %collective-permute-start.4 = (bf16[2,9,64,128]{3,2,1,0:T(8,128)(2,1)S(1)}, bf16[2,9,64,128]{3,2,1,0:T(8,128)(2,1)S(1)}, u32[]{:S(2)}, u32[]{:S(2)}) collective-permute-start(bf16[2,9,64,128]{3,2,1,0:T(8,128)(2,1)S(1)} %collective-permute-done.3.refs_3_), channel_id=1, source_target_pairs={{0,8},{1,9},{2,0},{3,1},{4,6},{5,7},{6,14},{7,15},{8,16},{9,17},{1... | collective-permute-start | bytes 884744 | tf_op jit(solution)/shard_map/ppermute | solution.py:631
  19.9 12.0 %collective-permute-start.6 = (bf16[32,4096]{1,0:T(8,128)(2,1)S(1)}, bf16[32,4096]{1,0:T(8,128)(2,1)S(1)}, u32[]{:S(2)}, u32[]{:S(2)}) collective-permute-start(bf16[32,4096]{1,0:T(8,128)(2,1)S(1)} %bitcast.4), channel_id=1, source_target_pairs={{1,0},{0,1},{3,2},{2,3},{5,4},{4,5},{7,6},{6,7},{9,8},{8,9},{11,10... | collective-permute-start | bytes 786440 | tf_op jit(solution)/shard_map/ppermute | solution.py:633
  31.9 6.0 %collective-permute-start.8 = (bf16[2,9,64,128]{3,2,1,0:T(8,128)(2,1)S(1)}, bf16[2,9,64,128]{3,2,1,0:T(8,128)(2,1)S(1)}, u32[]{:S(2)}, u32[]{:S(2)}) collective-permute-start(bf16[2,9,64,128]{3,2,1,0:T(8,128)(2,1)S(1)} %collective-permute-done.4.refs_7_.refs_2_), channel_id=1, source_target_pairs={{0,4},{1,5},{2,6},{3,7},{4,0},{5,1},{6,2},{7,3},{8,12},{9,13},{10,... | collective-permute-start | bytes 884744 | tf_op jit(solution)/shard_map/ppermute | solution.py:644
  32.0 6.7 %collective-permute-start.7 = (bf16[2,9,64,128]{3,2,1,0:T(8,128)(2,1)S(1)}, bf16[2,9,64,128]{3,2,1,0:T(8,128)(2,1)S(1)}, u32[]{:S(2)}, u32[]{:S(2)}) collective-permute-start(bf16[2,9,64,128]{3,2,1,0:T(8,128)(2,1)S(1)} %collective-permute-done.4.refs_7_.refs_2_), channel_id=1, source_target_pairs={{0,8},{1,9},{2,0},{3,1},{4,6},{5,7},{6,14},{7,15},{8,16},{9,17},{1... | collective-permute-start | bytes 884744 | tf_op jit(solution)/shard_map/ppermute | solution.py:643
  38.8 4.5 %collective-permute-start.10 = (bf16[2,9,64,128]{3,2,1,0:T(8,128)(2,1)S(1)}, bf16[2,9,64,128]{3,2,1,0:T(8,128)(2,1)S(1)}, u32[]{:S(2)}, u32[]{:S(2)}) collective-permute-start(bf16[2,9,64,128]{3,2,1,0:T(8,128)(2,1)S(1)} %collective-permute-done.7.refs_2_), channel_id=1, source_target_pairs={{0,4},{1,5},{2,6},{3,7},{4,0},{5,1},{6,2},{7,3},{8,12},{9,13},{10,... | collective-permute-start | bytes 884744 | tf_op jit(solution)/shard_map/ppermute | solution.py:644
  38.8 6.7 %collective-permute-start.9 = (bf16[2,9,64,128]{3,2,1,0:T(8,128)(2,1)S(1)}, bf16[2,9,64,128]{3,2,1,0:T(8,128)(2,1)S(1)}, u32[]{:S(2)}, u32[]{:S(2)}) collective-permute-start(bf16[2,9,64,128]{3,2,1,0:T(8,128)(2,1)S(1)} %collective-permute-done.7.refs_2_), channel_id=1, source_target_pairs={{0,8},{1,9},{2,0},{3,1},{4,6},{5,7},{6,14},{7,15},{8,16},{9,17},{1... | collective-permute-start | bytes 884744 | tf_op jit(solution)/shard_map/ppermute | solution.py:643
